TPU v7x, 32 devices: a whole 2x2x4 slice. The times are simulated.
32 devices in a mesh: req: 4 (over y, core), hid: 8 (over z, x).
Axes of the slice: x: 2, y: 2, z: 4, core: 2. Of those that a mesh axis runs over, the one named last changes fastest.
Arguments:
- tokens: bfloat16 [6144, 1536], P(('req', 'hid')), may hold values from -6 to 6
- segment: int32 [6144], P(('req', 'hid')), may hold values from 0 to 15, as said below
- attn_gain: float32 [1536], replicated, may hold values from 0.1 to 1.9
- w_query: bfloat16 [1536, 1536], replicated, may hold values from -0.2 to 0.2
- w_key: bfloat16 [1536, 512], replicated, may hold values from -0.2 to 0.2
- w_value: bfloat16 [1536, 512], replicated, may hold values from -0.15625 to 0.15625
- q_gain: float32 [64], replicated, may hold values from 0.5 to 6
- k_gain: float32 [64], replicated, may hold values from 0.5 to 6
- w_out: bfloat16 [1536, 1536], replicated, may hold values from -0.15625 to 0.15625
- ffn_gain: float32 [1536], replicated, may hold values from 0.1 to 1.9
- w_gate: bfloat16 [4608, 1536], P(('req', 'hid')), may hold values from -0.15625 to 0.15625
- w_up: bfloat16 [4608, 1536], P(('req', 'hid')), may hold values from -0.15625 to 0.15625
- w_down: bfloat16 [4608, 1536], P(('req', 'hid')), may hold values from -0.09375 to 0.09375
Outputs:
- mixed: bfloat16 [6144, 1536], P(('req', 'hid'))
- kv_cache: bfloat16 [6144, 1024], P(('req', 'hid'))
Inputs may be any that keep to these rules, and one draw needn't show every extreme that they name: Segment ids never fall along the tokens and start at 0. A segment never crosses a boundary between aligned blocks of 1536 tokens; the first block is one segment of exactly 1536 tokens, and every later block holds exactly five segments.
All inputs are finite; a program needn't handle non-finite values.
Results may differ from a plain program's by a relative error of at most 0.015.
Values may be sent and summed in bfloat16 or wider, within the bound.
A program may use at most 128 MiB of HBM per device.

v0:
```python
import jax
import jax.numpy as jnp
from jax import lax
from jax.sharding import PartitionSpec as P

H = 24
KVH = 8
HD = 64


EPSILON = 1e-05
ROPE_BASE = 1000000.0
NEG_FILL = -1e30
SCORE_SCALE = 0.125


def rms_scale(values, gain):
    mean_sq = jnp.mean(values * values, axis=-1, keepdims=True)
    return values * lax.rsqrt(mean_sq + EPSILON) * gain


def seg_positions(seg_ids):
    indices = jnp.arange(seg_ids.shape[0], dtype=jnp.int32)
    is_first = jnp.concatenate([jnp.ones((1,), bool), seg_ids[1:] != seg_ids[:-1]])
    seg_begin = lax.cummax(jnp.where(is_first, indices, jnp.zeros_like(indices)), axis=0)
    return indices - seg_begin


def rotate(heads, positions):
    half_dim = heads.shape[-1] // 2
    inv_freq = ROPE_BASE ** (-(jnp.arange(half_dim, dtype=jnp.float32) * 2.0) / (2.0 * half_dim))
    angles = positions.astype(jnp.float32)[:, None] * inv_freq[None, :]
    cos_val = jnp.cos(angles)[:, None, :]
    sin_val = jnp.sin(angles)[:, None, :]
    left = heads[..., :half_dim]
    right = heads[..., half_dim:]
    return jnp.concatenate(
        [left * cos_val - right * sin_val, right * cos_val + left * sin_val], axis=-1
    )


def block_length(shard_rows):
    return 4 * shard_rows


def key_block(running, key_blk, val_blk, key_seg, key_idx, q_grid, own_seg, query_idx):
    run_peak, run_total, run_acc = running
    k_grid = key_blk.reshape(-1, KVH, HD).transpose(1, 0, 2)
    v_grid = val_blk.reshape(-1, KVH, HD).transpose(1, 0, 2)
    scores = (
        jnp.einsum("kgqd,kcd->kgqc", q_grid, k_grid, preferred_element_type=jnp.float32)
        * SCORE_SCALE
    )
    allowed = (key_idx[None, :] <= query_idx[:, None]) & (key_seg[None, :] == own_seg[:, None])
    scores = jnp.where(allowed, scores, NEG_FILL)
    new_peak = jnp.maximum(run_peak, jnp.max(scores, axis=-1))
    weights = jnp.where(allowed, jnp.exp(scores - new_peak[..., None]), 0.0)
    factor = jnp.exp(run_peak - new_peak)
    new_total = run_total * factor + jnp.sum(weights, axis=-1)
    product = jnp.einsum(
        "kgqc,kcd->kgqd", weights.astype(jnp.bfloat16), v_grid, preferred_element_type=jnp.float32
    )
    return (new_peak, new_total, run_acc * factor[..., None] + product)


def unit_terms(pieces, gathered):
    gate_part, up_part, down_part = pieces
    contract = (((1,), (1,)), ((), ()))
    gate_act = lax.dot_general(gathered, gate_part, contract, preferred_element_type=jnp.float32)
    up_act = lax.dot_general(gathered, up_part, contract, preferred_element_type=jnp.float32)
    hidden = (jax.nn.silu(gate_act) * up_act).astype(jnp.bfloat16)
    return jnp.dot(hidden, down_part, preferred_element_type=jnp.float32)


def per_device(
    tokens,
    segment,
    attn_gain,
    w_query,
    w_key,
    w_value,
    q_gain,
    k_gain,
    w_out,
    ffn_gain,
    w_gate,
    w_up,
    w_down,
):
    shard_rows = tokens.shape[0]
    groups = H // KVH
    group_seg = lax.all_gather(segment, "hid", axis=0, tiled=True)
    row_base = lax.axis_index("hid") * shard_rows
    positions = lax.dynamic_slice_in_dim(seg_positions(group_seg), row_base, shard_rows)
    own_seg = lax.dynamic_slice_in_dim(group_seg, row_base, shard_rows)
    query_idx = row_base + jnp.arange(shard_rows, dtype=jnp.int32)
    resid = tokens.astype(jnp.float32)
    normed = rms_scale(resid, attn_gain).astype(jnp.bfloat16)
    q_raw = jnp.dot(normed, w_query, preferred_element_type=jnp.float32).reshape(shard_rows, H, HD)
    k_raw = jnp.dot(normed, w_key, preferred_element_type=jnp.float32).reshape(shard_rows, KVH, HD)
    queries = rotate(rms_scale(q_raw, q_gain), positions).astype(jnp.bfloat16)
    key_heads = (
        rotate(rms_scale(k_raw, k_gain), positions)
        .astype(jnp.bfloat16)
        .reshape(shard_rows, KVH * HD)
    )
    values = jnp.dot(normed, w_value, preferred_element_type=jnp.float32).astype(jnp.bfloat16)
    kv_cache = jnp.concatenate([key_heads, values], axis=1)
    q_grid = queries.reshape(shard_rows, KVH, groups, HD).transpose(1, 2, 0, 3)
    start_state = (
        jnp.full((KVH, groups, shard_rows), NEG_FILL, jnp.float32),
        jnp.zeros((KVH, groups, shard_rows), jnp.float32),
        jnp.zeros((KVH, groups, shard_rows, HD), jnp.float32),
    )
    key_part = lax.all_gather(key_heads, "hid", axis=0, tiled=True)
    val_part = lax.all_gather(values, "hid", axis=0, tiled=True)
    key_count = key_part.shape[0]
    blk_len = block_length(shard_rows)

    def one_block(block_idx, state_in):
        offset = jnp.asarray(block_idx, jnp.int32) * blk_len
        local_off = jnp.asarray(block_idx, jnp.int32) * blk_len
        key_blk = lax.dynamic_slice_in_dim(key_part, local_off, blk_len)
        val_blk = lax.dynamic_slice_in_dim(val_part, local_off, blk_len)
        key_seg = lax.dynamic_slice_in_dim(group_seg, offset, blk_len)
        key_idx = offset + jnp.arange(blk_len, dtype=jnp.int32)
        return key_block(state_in, key_blk, val_blk, key_seg, key_idx, q_grid, own_seg, query_idx)

    run_peak, run_total, run_acc = lax.fori_loop(0, key_count // blk_len, one_block, start_state)
    attended = (
        (run_acc / run_total[..., None])
        .transpose(2, 0, 1, 3)
        .reshape(shard_rows, H * HD)
        .astype(jnp.bfloat16)
    )
    after_attn = (resid + jnp.dot(attended, w_out, preferred_element_type=jnp.float32)).astype(
        jnp.bfloat16
    )
    after_f32 = lax.optimization_barrier(after_attn).astype(jnp.float32)
    mlp_in = rms_scale(after_f32, ffn_gain).astype(jnp.bfloat16)
    gathered = lax.all_gather(mlp_in, "hid", axis=0, tiled=True)
    unit_sum = unit_terms(
        (
            lax.all_gather(w_gate, "req", axis=0, tiled=True),
            lax.all_gather(w_up, "req", axis=0, tiled=True),
            lax.all_gather(w_down, "req", axis=0, tiled=True),
        ),
        gathered,
    )
    own_share = lax.psum_scatter(
        unit_sum.astype(jnp.bfloat16), "hid", scatter_dimension=0, tiled=True
    ).astype(jnp.float32)
    mixed = (after_f32 + own_share).astype(jnp.bfloat16)
    return (mixed, kv_cache)


def solution(mesh):
    placed = (
        P(("req", "hid"), None),
        P(("req", "hid")),
        P(),
        P(),
        P(),
        P(),
        P(),
        P(),
        P(),
        P(),
        P(("req", "hid"), None),
        P(("req", "hid"), None),
        P(("req", "hid"), None),
    )
    return jax.shard_map(
        per_device,
        mesh=mesh,
        in_specs=placed,
        out_specs=(P(("req", "hid"), None), P(("req", "hid"), None)),
        check_vma=False,
    )
```

profile of v0, /device:TPU:0, one launch (start us, length us, event | category | flops | bytes accessed | tf_op | source)
XLA Modules:
  0.0 420.7 jit_solution(10833466397497071258)
XLA Ops:
  10.2 13.2 %all-reduce = s32[1536]{0:T(1024)S(1)} all-reduce(s32[1536]{0:T(1024)S(1)} %dynamic-update-slice), channel_id=1, replica_groups=mesh['req'=4,'hid'=8] {'hid'}, use_global_device_ids=true, to_apply=%add | all-reduce | flops 1536 | bytes 12288
  25.4 1.9 multiply_reduce_fusion.1
  28.7 2.6 convolution_convert_fusion.1
  32.4 4.4 %fusion.26 = f32[192,1536]{0,1:T(8,128)S(1)} fusion(bf16[1536,1536]{1,0:T(8,128)(2,1)} %param.18, bf16[192,1536]{1,0:T(8,128)(2,1)S(1)} %copy-done.3, f32[1536]{0:T(1024)S(1)} %copy-done.8, f32[192]{0:T(256)S(1)} %add_rsqrt_fusion.3), kind=kOutput, calls=%fused_computation.66 | convolution fusion | flops 907149312 | bytes 6494976 | tf_op jit(solution)/shard_map/dot_general | solution.py:99
  38.7 32.5 %all-gather.7.cloned.1.call-done = bf16[1536,512]{1,0:T(8,128)(2,1)} async-done(((bf16[192,512]{1,0:T(8,128)(2,1)}), bf16[1536,512]{1,0:T(8,128)(2,1)}) %all-gather.7.cloned.1.call-update) | async-done | bytes 1572880 | tf_op jit(solution)/shard_map/all_gather | solution.py:115
  71.2 45.2 %all-gather.9.cloned.1.call-done = bf16[1536,512]{1,0:T(8,128)(2,1)} async-done(((bf16[192,512]{1,0:T(8,128)(2,1)}), bf16[1536,512]{1,0:T(8,128)(2,1)}) %all-gather.9.cloned.1.call-update) | async-done | bytes 1572880 | tf_op jit(solution)/shard_map/all_gather | solution.py:116
  116.4 58.0 %while.18 = (s32[]{:T(128)}, f32[8,3,192]{2,1,0:T(4,128)S(1)}, f32[8,3,192]{2,1,0:T(4,128)S(1)}, f32[8,3,192,64]{2,3,1,0:T(8,128)}, s32[1536]{0:T(1024)S(1)}, /*...) while((s32[]{:T(128)}, f32[8,3,192]{2,1,0:T(4,128)S(1)}, ...), condition=%wide.region_8.9_spmd.clone, body=%wide.region_5.0_spmd.clone.sunk | while | flops 953327040 | bytes 54183372 | solution.py:129
  116.7 2.4 constant_dynamic-slice_fusion.3
  120.5 8.9 %fusion.56 = (f32[8,3,192]{2,1,0:T(4,128)S(1)}, f32[8,768,3,192]{1,3,2,0:T(8,128)}) fusion(pred[192,768]{1,0:T(8,128)(4,1)S(1)} %compare_and_fusion.2, bf16[8,768,64,1]{1,2,3,0:T(8,128)(2,1)S(1)} %bitcast.75, bf16[8,3,192,64]{2,3,1,0:T(8,128)(2,1)} %get-tuple-element.382), kind=kOutput, calls=%fused_computation.3.clone.1 | convolution fusion | flops 463597056 | bytes 15697920 | tf_op jit(solution)/shard_map/while/body/eval_jaxpr/kgqd,kcd->kgqc/dot_general | solution.py:51
  129.4 7.6 %fusion.57 = f32[8,3,192]{2,1,0:T(4,128)S(1)} fusion(f32[8,768,3,192]{1,3,2,0:T(8,128)} %get-tuple-element.343, f32[8,3,192]{2,1,0:T(4,128)S(1)} %select_maximum_fusion.2, pred[192,768]{1,0:T(8,128)(4,1)S(1)} %compare_and_fusion.2), kind=kLoop, calls=%fused_computation.5.clone.1 | loop fusion | flops 17690112 | bytes 14340096 | tf_op jit(solution)/shard_map/while/body/eval_jaxpr/reduce_sum | solution.py:59
  137.4 7.9 %fusion.59 = f32[8,3,192,64]{2,3,1,0:T(8,128)} fusion(f32[8,3,192,64]{2,3,1,0:T(8,128)} %get-tuple-element.364, bf16[8,768,64,1]{1,2,3,0:T(8,128)(2,1)S(1)} %bitcast.76, f32[8,768,3,192]{1,3,2,0:T(8,128)} %get-tuple-element.343, f32[8,3,192]{2,1,0:T(4,128)S(1)} %select_maximum_fusion.2, pred[192,768]{1,0:T(8,128)(4,1)S(1)} %compare_and_fusion.2, ...), kind=kOutput, calls=%fused_computation.9.clone.1 | convolution fusion | flops 471564288 | bytes 17485824 | tf_op jit(solution)/shard_map/while/body/eval_jaxpr/kgqc,kcd->kgqd/dot_general | solution.py:60
  145.6 2.4 constant_dynamic-slice_fusion.3
  149.3 8.9 %fusion.56 = (f32[8,3,192]{2,1,0:T(4,128)S(1)}, f32[8,768,3,192]{1,3,2,0:T(8,128)}) fusion(pred[192,768]{1,0:T(8,128)(4,1)S(1)} %compare_and_fusion.2, bf16[8,768,64,1]{1,2,3,0:T(8,128)(2,1)S(1)} %bitcast.75, bf16[8,3,192,64]{2,3,1,0:T(8,128)(2,1)} %get-tuple-element.382), kind=kOutput, calls=%fused_computation.3.clone.1 | convolution fusion | flops 463597056 | bytes 15697920 | tf_op jit(solution)/shard_map/while/body/eval_jaxpr/kgqd,kcd->kgqc/dot_general | solution.py:51
  158.2 7.6 %fusion.57 = f32[8,3,192]{2,1,0:T(4,128)S(1)} fusion(f32[8,768,3,192]{1,3,2,0:T(8,128)} %get-tuple-element.343, f32[8,3,192]{2,1,0:T(4,128)S(1)} %select_maximum_fusion.2, pred[192,768]{1,0:T(8,128)(4,1)S(1)} %compare_and_fusion.2), kind=kLoop, calls=%fused_computation.5.clone.1 | loop fusion | flops 17690112 | bytes 14340096 | tf_op jit(solution)/shard_map/while/body/eval_jaxpr/reduce_sum | solution.py:59
  166.1 8.2 %fusion.59 = f32[8,3,192,64]{2,3,1,0:T(8,128)} fusion(f32[8,3,192,64]{2,3,1,0:T(8,128)} %get-tuple-element.364, bf16[8,768,64,1]{1,2,3,0:T(8,128)(2,1)S(1)} %bitcast.76, f32[8,768,3,192]{1,3,2,0:T(8,128)} %get-tuple-element.343, f32[8,3,192]{2,1,0:T(4,128)S(1)} %select_maximum_fusion.2, pred[192,768]{1,0:T(8,128)(4,1)S(1)} %compare_and_fusion.2, ...), kind=kOutput, calls=%fused_computation.9.clone.1 | convolution fusion | flops 471564288 | bytes 17485824 | tf_op jit(solution)/shard_map/while/body/eval_jaxpr/kgqc,kcd->kgqd/dot_general | solution.py:60
  174.4 1.6 divide_convert_fusion
  176.1 3.5 fusion.15
  182.3 77.6 %all-gather.11.cloned.1.call-done = bf16[1536,1536]{1,0:T(8,128)(2,1)} async-done(((bf16[192,1536]{1,0:T(8,128)(2,1)}), bf16[1536,1536]{1,0:T(8,128)(2,1)}) %all-gather.11.cloned.1.call-update) | async-done | bytes 4718608 | tf_op jit(solution)/shard_map/all_gather | solution.py:141
  259.9 7.6 %fusion.30 = f32[1536,576]{0,1:T(8,128)} fusion(bf16[1536,1536]{1,0:T(8,128)(2,1)} %all-gather.11.cloned.1.call-done, bf16[576,1536]{1,0:T(8,128)(2,1)} %all-gather.13.cloned.1.call-done), kind=kOutput, calls=%fused_computation.68 | convolution fusion | flops 2717908992 | bytes 10027008 | tf_op jit(solution)/shard_map/dot_general | solution.py:69
  267.5 12.7 %all-gather.15.cloned.1.call-done = bf16[576,1536]{1,0:T(8,128)(2,1)} async-done(((bf16[144,1536]{1,0:T(8,128)(2,1)}), bf16[576,1536]{1,0:T(8,128)(2,1)}) %all-gather.15.cloned.1.call-update) | async-done | bytes 1769488 | tf_op jit(solution)/shard_map/all_gather | solution.py:145
  280.2 22.2 %all-gather.17.cloned.1.call-done = bf16[576,1536]{1,0:T(8,128)(2,1)} async-done(((bf16[144,1536]{1,0:T(8,128)(2,1)}), bf16[576,1536]{1,0:T(8,128)(2,1)}) %all-gather.17.cloned.1.call-update) | async-done | bytes 1769488 | tf_op jit(solution)/shard_map/all_gather | solution.py:146
  302.4 13.8 %convolution_convert_fusion = bf16[1536,1536]{1,0:T(8,128)(2,1)} fusion(bf16[576,1536]{1,0:T(8,128)(2,1)} %all-gather.17.cloned.1.call-done, f32[1536,576]{0,1:T(8,128)} %fusion.30, bf16[1536,1536]{1,0:T(8,128)(2,1)} %all-gather.11.cloned.1.call-done, bf16[576,1536]{1,0:T(8,128)(2,1)} %all-gather.15.cloned.1.call-done), kind=kOutput, calls=%fused_computation.22 | convolution fusion | flops 5443485696 | bytes 16515072 | tf_op jit(solution)/shard_map/dot_general | solution.py:72
  318.0 93.8 %reduce-scatter.2.cloned.1.call-done = bf16[192,1536]{1,0:T(8,128)(2,1)} async-done(((bf16[1536,1536]{1,0:T(8,128)(2,1)}), bf16[192,1536]{1,0:T(8,128)(2,1)}) %reduce-scatter.2.cloned.1.call-update) | async-done | bytes 589840 | tf_op jit(solution)/shard_map/reduce_scatter | solution.py:150
  411.8 2.0 fusion.22
  (84 shorter events, 17.1 us)
Async XLA Ops:
  7.2 18.2 %copy-start = (bf16[1536,512]{1,0:T(8,128)(2,1)S(1)}, bf16[1536,512]{1,0:T(8,128)(2,1)}, u32[]{:S(2)}) copy-start(bf16[1536,512]{1,0:T(8,128)(2,1)} %param.19) | copy-start | bytes 4718596
  7.2 64.0 %all-gather.7.cloned.1.call-start = ((), (), s32[]{:S(2)}) async-start(), calls=%async_computation.1 | async-start | bytes 1769472 | tf_op jit(solution)/shard_map/all_gather | solution.py:115
  25.4 2.2 copy-start.6
  27.3 1.5 copy-start.3
  27.3 1.5 copy-start.8
  28.7 87.8 %all-gather.9.cloned.1.call-start = ((), (), s32[]{:S(2)}) async-start(), calls=%async_computation.2 | async-start | bytes 1769472 | tf_op jit(solution)/shard_map/all_gather | solution.py:116
  31.4 150.9 %all-gather.13.cloned.1.call-start = ((), (), s32[]{:S(2)}) async-start(), calls=%async_computation.4 | async-start | bytes 2211840 | tf_op jit(solution)/shard_map/all_gather | solution.py:144
  32.1 227.7 %all-gather.11.cloned.1.call-start = ((), (), s32[]{:S(2)}) async-start(), calls=%async_computation.3 | async-start | bytes 5308416 | tf_op jit(solution)/shard_map/all_gather | solution.py:141
  32.4 4.6 %copy-start.7 = (f32[64]{0:T(128)S(1)}, f32[64]{0:T(128)}, u32[]{:S(2)}) copy-start(f32[64]{0:T(128)} %param.21) | copy-start | bytes 772
  174.4 1.7 copy-start.4
  176.1 3.7 copy-start.5
  180.8 99.4 %all-gather.15.cloned.1.call-start = ((), (), s32[]{:S(2)}) async-start(), calls=%async_computation.5 | async-start | bytes 2211840 | tf_op jit(solution)/shard_map/all_gather | solution.py:145
  181.4 121.0 %all-gather.17.cloned.1.call-start = ((), (), s32[]{:S(2)}) async-start(), calls=%async_computation.6 | async-start | bytes 2211840 | tf_op jit(solution)/shard_map/all_gather | solution.py:146
  182.0 229.8 %reduce-scatter.2.cloned.1.call-start = ((), (), s32[]{:S(2)}) async-start(), calls=%async_computation.7 | async-start | bytes 5308416 | tf_op jit(solution)/shard_map/reduce_scatter | solution.py:150
  316.2 0.9 copy-start.1
  316.2 1.0 copy-start.2
Sparse Core Ops, SparseCore 0:
  28.8 42.3 all-gather.6
  73.4 42.9 all-gather.8
  118.0 19.5 all-gather.12
  180.9 78.8 all-gather.10
  261.3 18.8 all-gather.14
  281.6 20.7 all-gather.16
  316.4 95.3 reduce-scatter.1
where the time goes:
time: 421 us
  waiting for transfers between devices  286 us (68%)
  matrix products  67.7 us (16%)
  other arithmetic  25.6 us (6%)
  between operations  15 us (4%)
  blocking collectives  13.2 us (3%)
  local copies, waits for them, and re-layouts  12.6 us (3%)
    reduce_scatter x1, waiting for transfers between devices, per_device(): lax.psum_scatter(unit_sum.astype(jnp.bfloat16), 'hid', scatter_dimension=...  93.8 us
    all_gather x1, waiting for transfers between devices, per_device(): gathered = lax.all_gather(mlp_in, 'hid', axis=0, tiled=True)  77.6 us
    all_gather x1, waiting for transfers between devices, per_device(): val_part = lax.all_gather(values, 'hid', axis=0, tiled=True)  45.2 us
    all_gather x1, waiting for transfers between devices, per_device(): key_part = lax.all_gather(key_heads, 'hid', axis=0, tiled=True)  32.5 us
    all_gather x1, waiting for transfers between devices, per_device(): lax.all_gather(w_down, 'req', axis=0, tiled=True)  22.2 us
    dot_general x2, matrix products, key_block(): jnp.einsum('kgqd,kcd->kgqc', q_grid, k_grid, preferred_element_type=jnp.f...  17.8 us
    dot_general x2, matrix products, key_block(): jnp.einsum('kgqc,kcd->kgqd', weights.astype(jnp.bfloat16), v_grid, prefer...  16.1 us
    reduce_sum x2, other arithmetic, key_block(): new_total = run_total * factor + jnp.sum(weights, axis=-1)  15.2 us
  transfers between devices with their start and end apart: 7, of which 6 were waited for; matrix products, arithmetic and copies ran while one was open for 19% of the time, Pallas kernels for 0%

commit v1 on v0

v1 whole, which is shorter than its diff:
```python
import functools

import jax
import jax.numpy as jnp
from jax import lax
from jax.experimental import pallas as pl
from jax.experimental.pallas import tpu as pltpu
from jax.sharding import PartitionSpec as P

H = 24
KVH = 8
HD = 64


EPSILON = 1e-05
ROPE_BASE = 1000000.0
NEG_FILL = -1e30
SCORE_SCALE = 0.125
MESH = pl.DeviceIdType.MESH
F32 = jnp.float32
BF16 = jnp.bfloat16


def rms_scale(values, gain):
    mean_sq = jnp.mean(values * values, axis=-1, keepdims=True)
    return values * lax.rsqrt(mean_sq + EPSILON) * gain


def rotate(heads, positions):
    half_dim = heads.shape[-1] // 2
    inv_freq = ROPE_BASE ** (-(jnp.arange(half_dim, dtype=jnp.float32) * 2.0) / (2.0 * half_dim))
    angles = positions.astype(jnp.float32)[:, None] * inv_freq[None, :]
    cos_val = jnp.cos(angles)[:, None, :]
    sin_val = jnp.sin(angles)[:, None, :]
    left = heads[..., :half_dim]
    right = heads[..., half_dim:]
    return jnp.concatenate(
        [left * cos_val - right * sin_val, right * cos_val + left * sin_val], axis=-1
    )


def attention_kernel(q_ref, k_ref, v_ref, seg_ref, own_ref, base_ref, o_ref, bias_ref):
    rows, keys = bias_ref.shape

    @pl.when(pl.program_id(0) == 0)
    def _():
        q_idx = base_ref[0] + lax.broadcasted_iota(jnp.int32, (rows, keys), 0)
        k_idx = lax.broadcasted_iota(jnp.int32, (rows, keys), 1)
        allowed = (k_idx <= q_idx) & (seg_ref[...] == own_ref[...])
        bias_ref[...] = jnp.where(allowed, 0.0, NEG_FILL)

    k = k_ref[...]
    v = v_ref[...]
    for j in range(2):
        for g in range(H // KVH):
            c = (j * (H // KVH) + g) * HD
            q = q_ref[:, c : c + HD]
            zero = jnp.zeros_like(q)
            q = jnp.concatenate([q, zero] if j == 0 else [zero, q], axis=1)
            s = lax.dot_general(q, k, (((1,), (1,)), ((), ())), preferred_element_type=F32)
            s = s * SCORE_SCALE + bias_ref[...]
            p = jnp.exp(s - jnp.max(s, axis=-1, keepdims=True))
            total = jnp.sum(p, axis=-1, keepdims=True)
            o = jnp.dot(p.astype(BF16), v, preferred_element_type=F32)
            o_ref[:, c : c + HD] = (o[:, j * HD : (j + 1) * HD] / total).astype(BF16)


def attention(queries, kv_all, group_seg, own_seg, row_base):
    rows = queries.shape[0]
    keys = kv_all.shape[0]
    pairs = KVH // 2
    wide = 2 * (H // KVH) * HD
    return pl.pallas_call(
        attention_kernel,
        grid=(pairs,),
        out_shape=jax.ShapeDtypeStruct((rows, H * HD), BF16),
        in_specs=[
            pl.BlockSpec((rows, wide), lambda i: (0, i)),
            pl.BlockSpec((keys, 2 * HD), lambda i: (0, i)),
            pl.BlockSpec((keys, 2 * HD), lambda i: (0, i + pairs)),
            pl.BlockSpec((1, keys), lambda i: (0, 0)),
            pl.BlockSpec((rows, 1), lambda i: (0, 0)),
            pl.BlockSpec(memory_space=pltpu.SMEM),
        ],
        out_specs=pl.BlockSpec((rows, wide), lambda i: (0, i)),
        scratch_shapes=[pltpu.VMEM((rows, keys), F32)],
        compiler_params=pltpu.CompilerParams(vmem_limit_bytes=40 * 1024 * 1024),
        cost_estimate=pl.CostEstimate(
            flops=16 * rows * keys * H * HD,
            bytes_accessed=4 * rows * H * HD + 4 * keys * KVH * HD,
            transcendentals=rows * keys * H,
        ),
    )(
        queries,
        kv_all,
        kv_all,
        group_seg[None, :],
        own_seg[:, None],
        jnp.reshape(row_base, (1,)).astype(jnp.int32),
    )


def kv_gather_kernel(nz, kv_ref, out_ref, own_sem, right_s, right_r, left_s, left_r, side_s, side_r):
    req = lax.axis_index("req")
    hid = lax.axis_index("hid")
    x = lax.rem(hid, 2)
    z = hid // 2
    side = (req, hid + 1 - 2 * x)
    up = (req, lax.rem(hid + 2, 2 * nz))
    down = (req, lax.rem(hid + 2 * nz - 2, 2 * nz))
    barrier = pltpu.get_barrier_semaphore()
    pl.semaphore_signal(barrier, inc=1, device_id=side, device_id_type=MESH)

    @pl.when(z + 1 < nz)
    def _():
        pl.semaphore_signal(barrier, inc=1, device_id=up, device_id_type=MESH)

    @pl.when(z > 0)
    def _():
        pl.semaphore_signal(barrier, inc=1, device_id=down, device_id_type=MESH)

    pl.semaphore_wait(barrier, 1 + jnp.where(z + 1 < nz, 1, 0) + jnp.where(z > 0, 1, 0))

    def right(zb, s):
        slot = 2 * zb + x
        return pltpu.make_async_remote_copy(
            src_ref=kv_ref if s == 0 else out_ref.at[slot],
            dst_ref=out_ref.at[slot],
            send_sem=right_s.at[s],
            recv_sem=right_r.at[s],
            device_id=up,
            device_id_type=MESH,
        )

    def left(zb, s):
        slot = 2 * zb + x
        return pltpu.make_async_remote_copy(
            src_ref=kv_ref if s == 0 else out_ref.at[slot],
            dst_ref=out_ref.at[slot],
            send_sem=left_s.at[s],
            recv_sem=left_r.at[s],
            device_id=down,
            device_id_type=MESH,
        )

    def across(zb, own=False):
        slot = 2 * zb + x
        return pltpu.make_async_remote_copy(
            src_ref=kv_ref if own else out_ref.at[slot],
            dst_ref=out_ref.at[slot],
            send_sem=side_s.at[zb],
            recv_sem=side_r.at[zb],
            device_id=side,
            device_id_type=MESH,
        )

    for s in range(nz - 1):
        if s > 0:
            @pl.when(z - s >= 0)
            def _(s=s):
                right(z - s, s - 1).wait_recv()

            @pl.when(z + s < nz)
            def _(s=s):
                left(z + s, s - 1).wait_recv()

        @pl.when((z - s >= 0) & (z + 1 < nz))
        def _(s=s):
            right(z - s, s).start()

        @pl.when((z + s < nz) & (z > 0))
        def _(s=s):
            left(z + s, s).start()

        if s == 0:
            across(z, True).start()
            pltpu.make_async_copy(kv_ref, out_ref.at[hid], own_sem).start()
        else:

            @pl.when(z - s >= 0)
            def _(s=s):
                across(z - s).start()

            @pl.when(z + s < nz)
            def _(s=s):
                across(z + s).start()

    last = nz - 1

    @pl.when(z - last >= 0)
    def _():
        right(z - last, last - 1).wait_recv()
        across(z - last).start()

    @pl.when(z + last < nz)
    def _():
        left(z + last, last - 1).wait_recv()
        across(z + last).start()

    for s in range(nz - 1):

        @pl.when((z - s >= 0) & (z + 1 < nz))
        def _(s=s):
            right(z - s, s).wait_send()

        @pl.when((z + s < nz) & (z > 0))
        def _(s=s):
            left(z + s, s).wait_send()

    for zb in range(nz):
        across(zb).wait_send()
        across(zb).wait_recv()
    pltpu.make_async_copy(kv_ref, out_ref.at[hid], own_sem).wait()


def kv_gather(kv, hids):
    rows, cols = kv.shape
    nz = hids // 2
    dma = pltpu.SemaphoreType.DMA
    out = pl.pallas_call(
        functools.partial(kv_gather_kernel, nz),
        out_shape=jax.ShapeDtypeStruct((hids, rows, cols), BF16),
        in_specs=[pl.BlockSpec(memory_space=pltpu.VMEM)],
        out_specs=pl.BlockSpec(memory_space=pltpu.VMEM),
        scratch_shapes=[
            dma,
            dma((nz - 1,)),
            dma((nz - 1,)),
            dma((nz - 1,)),
            dma((nz - 1,)),
            dma((nz,)),
            dma((nz,)),
        ],
        compiler_params=pltpu.CompilerParams(
            collective_id=1, has_side_effects=True, vmem_limit_bytes=24 * 1024 * 1024
        ),
        cost_estimate=pl.CostEstimate(flops=0, bytes_accessed=100_000_000, transcendentals=0),
    )(kv)
    return out.reshape(hids * rows, cols)


def ffn_kernel(
    x_ref, after_ref, wg_ref, wu_ref, wd_ref, o_ref,
    gat, acc, sendc, rc, sd, rd, sx, rx, sy, ry, send_sem, recv_sem, own_sem,
):
    req = lax.axis_index("req")
    hid = lax.axis_index("hid")
    rows = x_ref.shape[0]
    half = rows // 2
    core = (req + 1 - 2 * lax.rem(req, 2), hid)
    ydev = (lax.rem(req + 2, 4), hid)
    xdev = (req, hid + 1 - 2 * lax.rem(hid, 2))
    lo, hi = pl.ds(0, half), pl.ds(half, half)

    barrier = pltpu.get_barrier_semaphore()
    for dev in (core, xdev, ydev):
        pl.semaphore_signal(barrier, inc=1, device_id=dev, device_id_type=MESH)
    pl.semaphore_wait(barrier, 3)

    def copy(src, dst, sem, dev):
        return pltpu.make_async_remote_copy(
            src_ref=src,
            dst_ref=dst,
            send_sem=send_sem.at[sem],
            recv_sem=recv_sem.at[sem],
            device_id=dev,
            device_id_type=MESH,
        )

    to_core = copy(x_ref, gat.at[0, 1], 0, core)
    x_lo = copy(x_ref.at[lo], gat.at[1, 0, lo], 1, xdev)
    x_hi = copy(x_ref.at[hi], gat.at[1, 0, hi], 2, xdev)
    y_lo = copy(x_ref.at[lo], gat.at[2, 0, lo], 3, ydev)
    y_hi = copy(x_ref.at[hi], gat.at[2, 0, hi], 4, ydev)
    d_lo = copy(gat.at[1, 0, lo], gat.at[3, 0, lo], 5, ydev)
    d_hi = copy(gat.at[2, 0, hi], gat.at[3, 0, hi], 6, xdev)
    core_x = copy(gat.at[1, 0], gat.at[1, 1], 7, core)
    core_y = copy(gat.at[2, 0], gat.at[2, 1], 8, core)
    core_d = copy(gat.at[3, 0], gat.at[3, 1], 9, core)
    sd_lo = copy(sd.at[lo], rd.at[lo], 10, xdev)
    sd_hi = copy(sd.at[hi], rd.at[hi], 11, ydev)
    sx_lo = copy(sx.at[lo], rx.at[lo], 12, xdev)
    sx_hi = copy(sx.at[hi], rx.at[hi], 13, xdev)
    sy_lo = copy(sy.at[lo], ry.at[lo], 14, ydev)
    sy_hi = copy(sy.at[hi], ry.at[hi], 15, ydev)

    def part(pair):
        return copy(sendc.at[pair], rc.at[pair], 16 + pair, core)

    x_lo.start()
    y_hi.start()
    x_hi.start()
    y_lo.start()
    to_core.start()
    own = pltpu.make_async_copy(x_ref, gat.at[0, 0], own_sem)
    own.start()

    def step(pair, carry):
        @pl.when(pair == 0)
        def _():
            own.wait()
            to_core.wait_recv()

        @pl.when(pair == 1)
        def _():
            x_lo.wait_recv()
            d_lo.start()
            y_hi.wait_recv()
            d_hi.start()
            x_hi.wait_recv()
            core_x.start()
            y_lo.wait_recv()
            core_y.start()
            core_x.wait_recv()

        @pl.when(pair == 2)
        def _():
            core_y.wait_recv()

        @pl.when(pair == 3)
        def _():
            d_lo.wait_recv()
            d_hi.wait_recv()
            core_d.start()
            core_d.wait_recv()

        x = gat[pair].reshape(2 * rows, gat.shape[-1])
        units = wg_ref.shape[0]
        cut = units // 3
        nt = (((1,), (1,)), ((), ()))
        total = None
        for j in range(3):
            at = pl.ds(j * cut, cut)
            gate = lax.dot_general(x, wg_ref[at, :], nt, preferred_element_type=F32)
            up = lax.dot_general(x, wu_ref[at, :], nt, preferred_element_type=F32)
            hidden = (gate / (1.0 + jnp.exp(-gate)) * up).astype(BF16)
            term = jnp.dot(hidden, wd_ref[at, :], preferred_element_type=F32)
            total = term if total is None else total + term
        acc[pair] = total[:rows]
        sendc[pair] = total[rows:].astype(BF16)
        part(pair).start()

        @pl.when(pair == 2)
        def _():
            part(1).wait_recv()
            sx[lo, :] = (acc[1, lo, :] + rc[1, lo, :].astype(F32)).astype(BF16)
            sx_lo.start()

        @pl.when(pair == 3)
        def _():
            part(2).wait_recv()
            sy[hi, :] = (acc[2, hi, :] + rc[2, hi, :].astype(F32)).astype(BF16)
            sy_hi.start()

        return carry

    lax.fori_loop(0, 4, step, 0)

    part(3).wait_recv()
    sd[...] = (acc[3] + rc[3].astype(F32)).astype(BF16)
    sd_lo.start()
    sd_hi.start()
    part(0).wait_recv()
    acc[0] = acc[0] + rc[0].astype(F32) + after_ref[...].astype(F32)
    sd_lo.wait_recv()
    sy[lo, :] = (acc[2, lo, :] + rc[2, lo, :].astype(F32) + rd[lo, :].astype(F32)).astype(BF16)
    sy_lo.start()
    sd_hi.wait_recv()
    sx[hi, :] = (acc[1, hi, :] + rc[1, hi, :].astype(F32) + rd[hi, :].astype(F32)).astype(BF16)
    sx_hi.start()
    sx_lo.wait_recv()
    sy_hi.wait_recv()
    sy_lo.wait_recv()
    sx_hi.wait_recv()
    o_ref[...] = (acc[0] + rx[...].astype(F32) + ry[...].astype(F32)).astype(BF16)
    for sent in (
        to_core, x_lo, x_hi, y_lo, y_hi, d_lo, d_hi, core_x, core_y, core_d,
        sd_lo, sd_hi, sx_lo, sx_hi, sy_lo, sy_hi, part(0), part(1), part(2), part(3),
    ):
        sent.wait_send()


def ffn_cube(mlp_in, after_attn, w_gate, w_up, w_down):
    rows, width = mlp_in.shape
    vmem = pl.BlockSpec(memory_space=pltpu.VMEM)
    block = pltpu.VMEM((rows, width), BF16)
    return pl.pallas_call(
        ffn_kernel,
        out_shape=jax.ShapeDtypeStruct((rows, width), BF16),
        in_specs=[vmem] * 5,
        out_specs=vmem,
        scratch_shapes=[
            pltpu.VMEM((4, 2, rows, width), BF16),
            pltpu.VMEM((4, rows, width), F32),
            pltpu.VMEM((4, rows, width), BF16),
            pltpu.VMEM((4, rows, width), BF16),
            block,
            block,
            block,
            block,
            block,
            block,
            pltpu.SemaphoreType.DMA((20,)),
            pltpu.SemaphoreType.DMA((20,)),
            pltpu.SemaphoreType.DMA,
        ],
        compiler_params=pltpu.CompilerParams(
            collective_id=2, has_side_effects=True, vmem_limit_bytes=56 * 1024 * 1024
        ),
        cost_estimate=pl.CostEstimate(
            flops=6 * 8 * rows * width * w_gate.shape[0],
            bytes_accessed=100_000_000,
            transcendentals=0,
        ),
    )(mlp_in, after_attn, w_gate, w_up, w_down)


def unit_terms(pieces, gathered):
    gate_part, up_part, down_part = pieces
    contract = (((1,), (1,)), ((), ()))
    gate_act = lax.dot_general(gathered, gate_part, contract, preferred_element_type=jnp.float32)
    up_act = lax.dot_general(gathered, up_part, contract, preferred_element_type=jnp.float32)
    hidden = (jax.nn.silu(gate_act) * up_act).astype(jnp.bfloat16)
    return jnp.dot(hidden, down_part, preferred_element_type=jnp.float32)


def per_device(
    cube,
    hids,
    tokens,
    segment,
    attn_gain,
    w_query,
    w_key,
    w_value,
    q_gain,
    k_gain,
    w_out,
    ffn_gain,
    w_gate,
    w_up,
    w_down,
):
    shard_rows = tokens.shape[0]
    if cube:
        lines = [list(range(x, hids, 2)) for x in range(2)]
        weights = [
            lax.all_gather(w, "hid", axis=0, tiled=True, axis_index_groups=lines)
            for w in (w_gate, w_up, w_down)
        ]
    else:
        weights = [lax.all_gather(w, "req", axis=0, tiled=True) for w in (w_gate, w_up, w_down)]
    group_seg = lax.all_gather(segment, "hid", axis=0, tiled=True)
    row_base = lax.axis_index("hid") * shard_rows
    own_seg = segment
    first = jnp.sum((group_seg[None, :] < own_seg[:, None]).astype(jnp.int32), axis=1)
    positions = row_base + jnp.arange(shard_rows, dtype=jnp.int32) - first
    resid = tokens.astype(jnp.float32)
    normed = rms_scale(resid, attn_gain).astype(jnp.bfloat16)
    q_raw = jnp.dot(normed, w_query, preferred_element_type=jnp.float32).reshape(shard_rows, H, HD)
    k_raw = jnp.dot(normed, w_key, preferred_element_type=jnp.float32).reshape(shard_rows, KVH, HD)
    queries = rotate(rms_scale(q_raw, q_gain), positions).astype(jnp.bfloat16)
    key_heads = (
        rotate(rms_scale(k_raw, k_gain), positions)
        .astype(jnp.bfloat16)
        .reshape(shard_rows, KVH * HD)
    )
    values = jnp.dot(normed, w_value, preferred_element_type=jnp.float32).astype(jnp.bfloat16)
    kv_cache = jnp.concatenate([key_heads, values], axis=1)
    if cube:
        kv_all = kv_gather(kv_cache, hids)
    else:
        kv_all = lax.all_gather(kv_cache, "hid", axis=0, tiled=True)
    attended = attention(
        queries.reshape(shard_rows, H * HD), kv_all, group_seg, own_seg, row_base
    )
    after_attn = (resid + jnp.dot(attended, w_out, preferred_element_type=jnp.float32)).astype(
        jnp.bfloat16
    )
    after_f32 = lax.optimization_barrier(after_attn).astype(jnp.float32)
    mlp_in = rms_scale(after_f32, ffn_gain).astype(jnp.bfloat16)
    if cube:
        return (ffn_cube(mlp_in, after_attn, *weights), kv_cache)
    gathered = lax.all_gather(mlp_in, "hid", axis=0, tiled=True)
    unit_sum = unit_terms(weights, gathered)
    own_share = lax.psum_scatter(
        unit_sum.astype(jnp.bfloat16), "hid", scatter_dimension=0, tiled=True
    ).astype(jnp.float32)
    mixed = (after_f32 + own_share).astype(jnp.bfloat16)
    return (mixed, kv_cache)


def solution(mesh):
    placed = (
        P(("req", "hid"), None),
        P(("req", "hid")),
        P(),
        P(),
        P(),
        P(),
        P(),
        P(),
        P(),
        P(),
        P(("req", "hid"), None),
        P(("req", "hid"), None),
        P(("req", "hid"), None),
    )
    cube = mesh.shape["req"] == 4 and mesh.shape["hid"] == 8
    return jax.shard_map(
        functools.partial(per_device, cube, mesh.shape["hid"]),
        mesh=mesh,
        in_specs=placed,
        out_specs=(P(("req", "hid"), None), P(("req", "hid"), None)),
        check_vma=False,
    )
```

time: 421 us -> 213 us (0.51)
  waiting for transfers between devices: 286 us -> 16.9 us
  Pallas kernels: 0 us -> 144 us
  matrix products: 67.7 us -> 10.5 us
  other arithmetic: 25.6 us -> 3.78 us
    all_gather x6 -> x3, waiting for transfers between devices: 190 us -> 14.8 us  [per_device(): lax.all_gather(w, 'hid', axis=0, tiled=True, axis_index_groups=lines)]
    pallas_call x0 -> x3, Pallas kernels: none -> 144 us  [the longest x1 73.1 us: kv_gather(): pl.pallas_call(functools.partial(kv_gather_kernel, nz), out_shape=jax.Sha...]
    reduce_scatter x1 -> x0, waiting for transfers between devices: 93.8 us -> none  [per_device(): lax.psum_scatter(unit_sum.astype(jnp.bfloat16), 'hid', scatter_dimension=...]
    dot_general x6 -> x0, matrix products: 55.3 us -> none  [the longest x2 17.8 us: key_block(): jnp.einsum('kgqd,kcd->kgqc', q_grid, k_grid, preferred_element_type=jnp.f...]
    reduce_sum x2 -> x1, other arithmetic: 15.2 us -> 0.94 us  [per_device(): jnp.sum((group_seg[None, :] < own_seg[:, None]).astype(jnp.int32), axis=1)]
    dynamic_slice x9 -> x0, local copies, waits for them, and re-layouts: 8.34 us -> none  [the longest x4 5.29 us: one_block(): val_blk = lax.dynamic_slice_in_dim(val_part, local_off, blk_len)]
    unnamed x21 -> x28, local copies, waits for them, and re-layouts: 3.28 us -> 8.33 us
  transfers between devices with their start and end apart: 7 -> 3, of which waited for: 6 -> 1; matrix products, arithmetic and copies ran while one was open for 19% -> 8% of each run, Pallas kernels for 0% -> 41%
where the time goes in v1:
time: 213 us
  Pallas kernels  144 us (68%)
  waiting for transfers between devices  16.9 us (8%)
  between operations  14.7 us (7%)
  blocking collectives  13.7 us (6%)
  matrix products  10.5 us (5%)
  local copies, waits for them, and re-layouts  8.83 us (4%)
  other arithmetic  3.78 us (2%)
    pallas_call x1, Pallas kernels, kv_gather(): pl.pallas_call(functools.partial(kv_gather_kernel, nz), out_shape=jax.Sha...  73.1 us
    pallas_call x1, Pallas kernels, ffn_cube(): pl.pallas_call(ffn_kernel, out_shape=jax.ShapeDtypeStruct((rows, width),...  56.1 us
    pallas_call x1, Pallas kernels, attention(): pl.pallas_call(attention_kernel, grid=(pairs,), out_shape=jax.ShapeDtypeS...  14.8 us
    all_gather x3, waiting for transfers between devices, per_device(): lax.all_gather(w, 'hid', axis=0, tiled=True, axis_index_groups=lines)  14.8 us
    unnamed x1, blocking collectives  13.7 us
    unnamed x28, local copies, waits for them, and re-layouts  8.33 us
    dot_general x1, matrix products, per_device(): jnp.dot(normed, w_query, preferred_element_type=jnp.float32)  4.34 us
  transfers between devices with their start and end apart: 3, of which 1 were waited for; matrix products, arithmetic and copies ran while one was open for 8% of the time, Pallas kernels for 41%

profile of v1, /device:TPU:0, one launch (start us, length us, event | category | flops | bytes accessed | tf_op | source)
XLA Modules:
  0.0 212.6 jit_solution(17974556370553300323)
XLA Ops:
  7.2 0.7 all-gather.4.cloned.1.call-update
  8.0 0.7 all-gather.6.cloned.1.call-update
  8.7 0.7 all-gather.8.cloned.1.call-update
  9.4 1.2 dynamic-slice
  11.4 0.9 dynamic-update-slice
  12.2 13.7 %all-reduce = s32[1536]{0:T(1024)S(1)} all-reduce(s32[1536]{0:T(1024)S(1)} %dynamic-update-slice), channel_id=1, replica_groups=mesh['req'=4,'hid'=8] {'hid'}, use_global_device_ids=true, to_apply=%add | all-reduce | flops 1536 | bytes 12288
  25.9 0.9 convert_reduce_fusion
  27.1 0.8 multiply_reduce_fusion.1
  28.5 1.9 convolution_convert_fusion
  30.5 73.1 %shard_map.140 = bf16[8,192,1024]{2,1,0:T(8,128)(2,1)S(1)} custom-call(bf16[192,1024]{1,0:T(8,128)(2,1)S(1)} %pad_maximum_fusion.1.kv_ref), custom_call_target="tpu_custom_call" | custom-call | bytes 100000000 | tf_op jit(solution)/shard_map/pallas_call | solution.py:220
  103.7 1.6 copy-done.1
  105.3 4.3 %fusion.10 = f32[192,1536]{0,1:T(8,128)S(1)} fusion(bf16[1536,1536]{1,0:T(8,128)(2,1)} %param.16, bf16[192,1536]{1,0:T(8,128)(2,1)S(1)} %copy-done.5, f32[1536]{0:T(1024)S(1)} %copy-done.11, f32[192]{0:T(256)S(1)} %add_rsqrt_fusion.3), kind=kOutput, calls=%fused_computation.34 | convolution fusion | flops 907149312 | bytes 6494976 | tf_op jit(solution)/shard_map/dot_general | solution.py:460
  109.9 0.4 copy-done.10
  110.3 0.3 multiply_multiply_fusion
  110.7 0.3 subtract_convert_fusion
  111.1 0.3 copy.23.q_ref
  111.3 0.3 copy-done.7
  111.7 1.9 copy-done.2
  113.6 14.8 %shard_map.141 = bf16[192,1536]{1,0:T(8,128)(2,1)S(1)} custom-call(bf16[192,1536]{1,0:T(8,128)(2,1)S(1)} %copy.23.q_ref, bf16[1536,1024]{1,0:T(8,128)(2,1)S(1)} %bitcast.15, bf16[1536,1024]{1,0:T(8,128)(2,1)S(1)} %bitcast.16, s32[1,1536]{1,0:T(1,128)S(1)} %broadcast_in_dim.4.seg_ref, s32[192,1]{1,0:T(8,128)S(1)} %copy.24.own_ref, s32[1]{0:T(128)} %bitcast.7.base_ref), custom_call_target="tpu_custom_call" | custom-call | flops 7247757312 | bytes 4325376 | tf_op jit(solution)/shard_map/pallas_call | solution.py:73
  128.5 3.4 %fusion.after_ref = bf16[192,1536]{1,0:T(8,128)(2,1)S(1)} fusion(bf16[192,1536]{1,0:T(8,128)(2,1)S(1)} %shard_map.141, bf16[1536,1536]{1,0:T(8,128)(2,1)} %param.21, bf16[192,1536]{1,0:T(8,128)(2,1)S(1)} %copy-done.6), kind=kOutput, calls=%fused_computation.1 | convolution fusion | flops 906854400 | bytes 6488064 | tf_op jit(solution)/shard_map/dot_general | solution.py:477
  132.2 1.0 fusion.3.x_ref
  133.2 14.8 %all-gather.8.cloned.1.call-done.wd_ref = bf16[576,1536]{1,0:T(8,128)(2,1)} async-done(((bf16[144,1536]{1,0:T(8,128)(2,1)}), bf16[576,1536]{1,0:T(8,128)(2,1)}) %all-gather.8.cloned.1.call-update) | async-done | bytes 1769488 | tf_op jit(solution)/shard_map/all_gather | solution.py:448
  148.0 56.1 %shard_map.142 = bf16[192,1536]{1,0:T(8,128)(2,1)} custom-call(bf16[192,1536]{1,0:T(8,128)(2,1)} %fusion.3.x_ref, bf16[192,1536]{1,0:T(8,128)(2,1)} %copy-done.4, bf16[576,1536]{1,0:T(8,128)(2,1)} %all-gather.4.cloned.1.call-done.wg_ref, bf16[576,1536]{1,0:T(8,128)(2,1)} %all-gather.6.cloned.1.call-done.wu_ref, ...), custom_call_target="tpu_custom_call" | custom-call | flops 8153726976 | bytes 100000000 | tf_op jit(solution)/shard_map/pallas_call | solution.py:387
  204.2 1.9 copy.29
  (44 shorter events, 1.7 us)
Async XLA Ops:
  7.2 19.9 %copy-start = (bf16[1536,512]{1,0:T(8,128)(2,1)S(1)}, bf16[1536,512]{1,0:T(8,128)(2,1)}, u32[]{:S(2)}) copy-start(bf16[1536,512]{1,0:T(8,128)(2,1)} %param.17) | copy-start | bytes 4718596
  7.2 19.7 %copy-start.5 = (bf16[192,1536]{1,0:T(8,128)(2,1)S(1)}, bf16[192,1536]{1,0:T(8,128)(2,1)}, u32[]{:S(2)}) copy-start(bf16[192,1536]{1,0:T(8,128)(2,1)} %param.13) | copy-start | bytes 1769476
  7.2 19.9 %copy-start.11 = (f32[1536]{0:T(1024)S(1)}, f32[1536]{0:T(1024)}, u32[]{:S(2)}) copy-start(f32[1536]{0:T(1024)} %param.15) | copy-start | bytes 18436
  7.2 126.0 %all-gather.4.cloned.1.call-start = ((), (), s32[]{:S(2)}) async-start(), calls=%async_computation | async-start | bytes 2211840 | tf_op jit(solution)/shard_map/all_gather | solution.py:448
  7.9 125.3 %all-gather.6.cloned.1.call-start = ((), (), s32[]{:S(2)}) async-start(), calls=%async_computation.1 | async-start | bytes 2211840 | tf_op jit(solution)/shard_map/all_gather | solution.py:448
  8.7 139.3 %all-gather.8.cloned.1.call-start = ((), (), s32[]{:S(2)}) async-start(), calls=%async_computation.2 | async-start | bytes 2211840 | tf_op jit(solution)/shard_map/all_gather | solution.py:448
  27.1 1.0 copy-start.9
  30.5 73.1 %copy-start.3 = (bf16[192,1024]{1,0:T(8,128)(2,1)}, bf16[192,1024]{1,0:T(8,128)(2,1)S(1)}, u32[]{:S(2)}) copy-start(bf16[192,1024]{1,0:T(8,128)(2,1)S(1)} %pad_maximum_fusion.1.kv_ref) | copy-start | bytes 1179652
  103.7 1.6 copy-start.1
  109.6 0.7 copy-start.10
  110.9 0.7 copy-start.7
  111.7 1.9 copy-start.2
  113.6 14.9 %copy-start.6 = (bf16[192,1536]{1,0:T(8,128)(2,1)S(1)}, bf16[192,1536]{1,0:T(8,128)(2,1)}, u32[]{:S(2)}) copy-start(bf16[192,1536]{1,0:T(8,128)(2,1)} %param.13) | copy-start | bytes 1769476
  128.5 3.7 %copy-start.8 = (f32[1536]{0:T(1024)S(1)}, f32[1536]{0:T(1024)}, u32[]{:S(2)}) copy-start(f32[1536]{0:T(1024)} %param.22) | copy-start | bytes 18436
  131.9 16.1 %copy-start.4 = (bf16[192,1536]{1,0:T(8,128)(2,1)}, bf16[192,1536]{1,0:T(8,128)(2,1)S(1)}, u32[]{:S(2)}) copy-start(bf16[192,1536]{1,0:T(8,128)(2,1)S(1)} %fusion.after_ref) | copy-start | bytes 1769476
Sparse Core Ops, SparseCore 0:
  9.6 52.5 all-gather.3
  63.8 43.0 all-gather.5
  108.5 39.5 all-gather.7

commit v2 on v1

v2 whole, which is shorter than its diff:
```python
import functools

import jax
import jax.numpy as jnp
from jax import lax
from jax.experimental import pallas as pl
from jax.experimental.pallas import tpu as pltpu
from jax.sharding import PartitionSpec as P

H = 24
KVH = 8
HD = 64


EPSILON = 1e-05
ROPE_BASE = 1000000.0
NEG_FILL = -1e30
SCORE_SCALE = 0.125
MESH = pl.DeviceIdType.MESH
F32 = jnp.float32
BF16 = jnp.bfloat16


def rms_scale(values, gain):
    mean_sq = jnp.mean(values * values, axis=-1, keepdims=True)
    return values * lax.rsqrt(mean_sq + EPSILON) * gain


def rotate(heads, positions):
    half_dim = heads.shape[-1] // 2
    inv_freq = ROPE_BASE ** (-(jnp.arange(half_dim, dtype=jnp.float32) * 2.0) / (2.0 * half_dim))
    angles = positions.astype(jnp.float32)[:, None] * inv_freq[None, :]
    cos_val = jnp.cos(angles)[:, None, :]
    sin_val = jnp.sin(angles)[:, None, :]
    left = heads[..., :half_dim]
    right = heads[..., half_dim:]
    return jnp.concatenate(
        [left * cos_val - right * sin_val, right * cos_val + left * sin_val], axis=-1
    )


def seg_gather_kernel(hids, seg_ref, out_ref, own_sem, send_sem, recv_sem):
    req = lax.axis_index("req")
    hid = lax.axis_index("hid")
    barrier = pltpu.get_barrier_semaphore()
    peers = [(req, lax.rem(hid + k, hids)) for k in range(1, hids)]
    for dev in peers:
        pl.semaphore_signal(barrier, inc=1, device_id=dev, device_id_type=MESH)
    own = pltpu.make_async_copy(seg_ref, out_ref.at[hid], own_sem)
    own.start()
    pl.semaphore_wait(barrier, hids - 1)
    copies = [
        pltpu.make_async_remote_copy(
            src_ref=seg_ref,
            dst_ref=out_ref.at[hid],
            send_sem=send_sem.at[k],
            recv_sem=recv_sem.at[k],
            device_id=dev,
            device_id_type=MESH,
        )
        for k, dev in enumerate(peers)
    ]
    for c in copies:
        c.start()
    for c in copies:
        c.wait()
    own.wait()


def seg_gather(segment, hids):
    rows = segment.shape[0]
    vmem = pl.BlockSpec(memory_space=pltpu.VMEM)
    out = pl.pallas_call(
        functools.partial(seg_gather_kernel, hids),
        out_shape=jax.ShapeDtypeStruct((hids, 1, rows), jnp.int32),
        in_specs=[vmem],
        out_specs=vmem,
        scratch_shapes=[
            pltpu.SemaphoreType.DMA,
            pltpu.SemaphoreType.DMA((hids - 1,)),
            pltpu.SemaphoreType.DMA((hids - 1,)),
        ],
        compiler_params=pltpu.CompilerParams(collective_id=1, has_side_effects=True),
    )(segment[None, :])
    return out.reshape(hids * rows)


def layer_kernel(
    q_ref, kv_ref, tok_ref, seg_ref, own_ref, gain_ref, wo_hbm, wg_hbm, wu_hbm, wd_hbm, o_ref,
    kvs, bias_ref, att, wo, wts, x_ref, after_ref,
    gat, acc, sendc, rc, sd, rd, sx, rx, sy, ry,
    send_sem, recv_sem, own_sem, w_send, w_recv, w_own,
    right_s, right_r, left_s, left_r, side_s, side_r,
):
    nz = 4
    req = lax.axis_index("req")
    hid = lax.axis_index("hid")
    x = lax.rem(hid, 2)
    z = hid // 2
    rows = q_ref.shape[0]
    keys = seg_ref.shape[1]
    half = rows // 2
    lo, hi = pl.ds(0, half), pl.ds(half, half)
    core = (req + 1 - 2 * lax.rem(req, 2), hid)
    ydev = (lax.rem(req + 2, 4), hid)
    xdev = (req, hid + 1 - 2 * x)
    zdev = (req, hid + 2 - 4 * lax.rem(z, 2))
    mirror = (req, 2 * (nz - 1 - z) + x)
    up = (req, lax.rem(hid + 2, 2 * nz))
    down = (req, lax.rem(hid + 2 * nz - 2, 2 * nz))

    barrier = pltpu.get_barrier_semaphore()
    for dev in (core, xdev, ydev, zdev, mirror):
        pl.semaphore_signal(barrier, inc=1, device_id=dev, device_id_type=MESH)
    load_wo = pltpu.make_async_copy(wo_hbm, wo, own_sem.at[0])
    load_wo.start()
    pl.semaphore_wait(barrier, 5)

    def remote(src, dst, s_sem, r_sem, dev):
        return pltpu.make_async_remote_copy(
            src_ref=src,
            dst_ref=dst,
            send_sem=s_sem,
            recv_sem=r_sem,
            device_id=dev,
            device_id_type=MESH,
        )

    def right(zb, s):
        slot = 2 * zb + x
        src = kv_ref if s == 0 else kvs.at[slot]
        return remote(src, kvs.at[slot], right_s.at[s], right_r.at[s], up)

    def left(zb, s):
        slot = 2 * zb + x
        src = kv_ref if s == 0 else kvs.at[slot]
        return remote(src, kvs.at[slot], left_s.at[s], left_r.at[s], down)

    def across(zb, own=False):
        slot = 2 * zb + x
        src = kv_ref if own else kvs.at[slot]
        return remote(src, kvs.at[slot], side_s.at[zb], side_r.at[zb], xdev)

    units = wg_hbm.shape[0]
    part_of = [pl.ds(k * units, units) for k in range(4)]
    w_local, w_y, w_z, w_zy = [], [], [], []
    for w, src in enumerate((wg_hbm, wu_hbm, wd_hbm)):
        w_local.append(pltpu.make_async_copy(src, wts.at[w, part_of[0]], w_own.at[w]))
        w_y.append(remote(src, wts.at[w, part_of[1]], w_send.at[3 * w], w_recv.at[3 * w], ydev))
        w_z.append(
            remote(src, wts.at[w, part_of[2]], w_send.at[3 * w + 1], w_recv.at[3 * w + 1], mirror)
        )
        w_zy.append(
            remote(
                wts.at[w, part_of[2]],
                wts.at[w, part_of[3]],
                w_send.at[3 * w + 2],
                w_recv.at[3 * w + 2],
                ydev,
            )
        )

    own_kv = pltpu.make_async_copy(kv_ref, kvs.at[hid], own_sem.at[1])
    for s in range(nz - 1):
        if s > 0:
            @pl.when(z - s >= 0)
            def _(s=s):
                right(z - s, s - 1).wait_recv()

            @pl.when(z + s < nz)
            def _(s=s):
                left(z + s, s - 1).wait_recv()

        @pl.when((z - s >= 0) & (z + 1 < nz))
        def _(s=s):
            right(z - s, s).start()

        @pl.when((z + s < nz) & (z > 0))
        def _(s=s):
            left(z + s, s).start()

        if s == 0:
            across(z, True).start()
            own_kv.start()
            for w in range(3):
                w_y[w].start()
        else:

            @pl.when(z - s >= 0)
            def _(s=s):
                across(z - s).start()

            @pl.when(z + s < nz)
            def _(s=s):
                across(z + s).start()

        w_z[s].start()
        w_local[s].start()
        if s == 0:
            q_idx = hid * rows + lax.broadcasted_iota(jnp.int32, (rows, keys), 0)
            k_idx = lax.broadcasted_iota(jnp.int32, (rows, keys), 1)
            allowed = (k_idx <= q_idx) & (seg_ref[...] == own_ref[...])
            bias_ref[...] = jnp.where(allowed, 0.0, NEG_FILL)

    last = nz - 1

    @pl.when(z - last >= 0)
    def _():
        right(z - last, last - 1).wait_recv()
        across(z - last).start()

    @pl.when(z + last < nz)
    def _():
        left(z + last, last - 1).wait_recv()
        across(z + last).start()

    w_z[0].wait_recv()
    w_zy[0].start()
    for zb in range(nz):
        across(zb).wait_recv()
    own_kv.wait()

    groups = H // KVH
    wide = 2 * groups * HD

    def heads(i, carry):
        k_at = pl.ds(pl.multiple_of(i * 2 * HD, 2 * HD), 2 * HD)
        v_at = pl.ds(pl.multiple_of(i * 2 * HD + KVH * HD, 2 * HD), 2 * HD)
        q_at = pl.ds(pl.multiple_of(i * wide, wide), wide)
        k = kvs[:, :, k_at].reshape(keys, 2 * HD)
        v = kvs[:, :, v_at].reshape(keys, 2 * HD)
        q_all = q_ref[:, q_at]
        outs = []
        for j in range(2):
            for g in range(groups):
                c = (j * groups + g) * HD
                q = q_all[:, c : c + HD]
                zero = jnp.zeros_like(q)
                q = jnp.concatenate([q, zero] if j == 0 else [zero, q], axis=1)
                s = lax.dot_general(q, k, (((1,), (1,)), ((), ())), preferred_element_type=F32)
                s = s * SCORE_SCALE + bias_ref[...]
                p = jnp.exp(s - jnp.max(s, axis=-1, keepdims=True))
                total = jnp.sum(p, axis=-1, keepdims=True)
                o = jnp.dot(p.astype(BF16), v, preferred_element_type=F32)
                outs.append((o[:, j * HD : (j + 1) * HD] / total).astype(BF16))
        att[:, q_at] = jnp.concatenate(outs, axis=1)

        @pl.when(i == 1)
        def _():
            w_z[1].wait_recv()
            w_zy[1].start()

        return carry

    lax.fori_loop(0, KVH // 2, heads, 0)

    load_wo.wait()
    after = tok_ref[...].astype(F32) + jnp.dot(att[...], wo[...], preferred_element_type=F32)
    after_ref[...] = after.astype(BF16)
    after = after_ref[...].astype(F32)
    mean_sq = jnp.mean(after * after, axis=-1, keepdims=True)
    x_ref[...] = (after * lax.rsqrt(mean_sq + EPSILON) * gain_ref[...]).astype(BF16)

    def copy(src, dst, sem, dev):
        return remote(src, dst, send_sem.at[sem], recv_sem.at[sem], dev)

    to_core = copy(x_ref, gat.at[0, 1], 0, core)
    x_lo = copy(x_ref.at[lo], gat.at[1, 0, lo], 1, xdev)
    x_hi = copy(x_ref.at[hi], gat.at[1, 0, hi], 2, xdev)
    y_lo = copy(x_ref.at[lo], gat.at[2, 0, lo], 3, zdev)
    y_hi = copy(x_ref.at[hi], gat.at[2, 0, hi], 4, zdev)
    d_lo = copy(gat.at[1, 0, lo], gat.at[3, 0, lo], 5, zdev)
    d_hi = copy(gat.at[2, 0, hi], gat.at[3, 0, hi], 6, xdev)
    core_x = copy(gat.at[1, 0], gat.at[1, 1], 7, core)
    core_y = copy(gat.at[2, 0], gat.at[2, 1], 8, core)
    core_d = copy(gat.at[3, 0], gat.at[3, 1], 9, core)
    sd_lo = copy(sd.at[lo], rd.at[lo], 10, xdev)
    sd_hi = copy(sd.at[hi], rd.at[hi], 11, zdev)
    sx_lo = copy(sx.at[lo], rx.at[lo], 12, xdev)
    sx_hi = copy(sx.at[hi], rx.at[hi], 13, xdev)
    sy_lo = copy(sy.at[lo], ry.at[lo], 14, zdev)
    sy_hi = copy(sy.at[hi], ry.at[hi], 15, zdev)

    def part(pair):
        return copy(sendc.at[pair], rc.at[pair], 16 + pair, core)

    x_lo.start()
    y_hi.start()
    x_hi.start()
    y_lo.start()
    to_core.start()
    own = pltpu.make_async_copy(x_ref, gat.at[0, 0], own_sem.at[2])
    own.start()
    w_z[2].wait_recv()
    w_zy[2].start()

    def step(pair, carry):
        @pl.when(pair == 0)
        def _():
            x_lo.wait_recv()
            d_lo.start()
            y_hi.wait_recv()
            d_hi.start()
            own.wait()
            to_core.wait_recv()
            for w in range(3):
                w_local[w].wait()
                w_y[w].wait_recv()
                w_zy[w].wait_recv()

        @pl.when(pair == 1)
        def _():
            x_hi.wait_recv()
            core_x.start()
            y_lo.wait_recv()
            core_y.start()
            core_x.wait_recv()

        @pl.when(pair == 2)
        def _():
            d_lo.wait_recv()
            d_hi.wait_recv()
            core_d.start()
            core_y.wait_recv()

        @pl.when(pair == 3)
        def _():
            core_d.wait_recv()

        xs = gat[pair].reshape(2 * rows, gat.shape[-1])
        cut = wts.shape[1] // 3
        nt = (((1,), (1,)), ((), ()))
        total = None
        for j in range(3):
            at = pl.ds(j * cut, cut)
            gate = lax.dot_general(xs, wts[0, at, :], nt, preferred_element_type=F32)
            up_act = lax.dot_general(xs, wts[1, at, :], nt, preferred_element_type=F32)
            hidden = (gate / (1.0 + jnp.exp(-gate)) * up_act).astype(BF16)
            term = jnp.dot(hidden, wts[2, at, :], preferred_element_type=F32)
            total = term if total is None else total + term
        acc[pair] = total[:rows]
        sendc[pair] = total[rows:].astype(BF16)
        part(pair).start()

        @pl.when(pair == 2)
        def _():
            part(1).wait_recv()
            sx[lo, :] = (acc[1, lo, :] + rc[1, lo, :].astype(F32)).astype(BF16)
            sx_lo.start()

        @pl.when(pair == 3)
        def _():
            part(2).wait_recv()
            sy[hi, :] = (acc[2, hi, :] + rc[2, hi, :].astype(F32)).astype(BF16)
            sy_hi.start()

        return carry

    lax.fori_loop(0, 4, step, 0)

    part(3).wait_recv()
    sd[...] = (acc[3] + rc[3].astype(F32)).astype(BF16)
    sd_lo.start()
    sd_hi.start()
    part(0).wait_recv()
    acc[0] = acc[0] + rc[0].astype(F32) + after_ref[...].astype(F32)
    sd_lo.wait_recv()
    sy[lo, :] = (acc[2, lo, :] + rc[2, lo, :].astype(F32) + rd[lo, :].astype(F32)).astype(BF16)
    sy_lo.start()
    sd_hi.wait_recv()
    sx[hi, :] = (acc[1, hi, :] + rc[1, hi, :].astype(F32) + rd[hi, :].astype(F32)).astype(BF16)
    sx_hi.start()
    sx_lo.wait_recv()
    sy_hi.wait_recv()
    sy_lo.wait_recv()
    sx_hi.wait_recv()
    o_ref[...] = (acc[0] + rx[...].astype(F32) + ry[...].astype(F32)).astype(BF16)

    for s in range(nz - 1):

        @pl.when((z - s >= 0) & (z + 1 < nz))
        def _(s=s):
            right(z - s, s).wait_send()

        @pl.when((z + s < nz) & (z > 0))
        def _(s=s):
            left(z + s, s).wait_send()

    for zb in range(nz):
        across(zb).wait_send()
    for sent in (
        to_core, x_lo, x_hi, y_lo, y_hi, d_lo, d_hi, core_x, core_y, core_d,
        sd_lo, sd_hi, sx_lo, sx_hi, sy_lo, sy_hi, part(0), part(1), part(2), part(3),
        *w_y, *w_z, *w_zy,
    ):
        sent.wait_send()


def layer(queries, kv, tokens, group_seg, own_seg, ffn_gain, w_out, w_gate, w_up, w_down):
    rows, width = tokens.shape
    keys = group_seg.shape[0]
    vmem = pl.BlockSpec(memory_space=pltpu.VMEM)
    hbm = pl.BlockSpec(memory_space=pl.ANY)
    dma = pltpu.SemaphoreType.DMA
    block = pltpu.VMEM((rows, width), BF16)
    blocks = pltpu.VMEM((4, rows, width), BF16)
    return pl.pallas_call(
        layer_kernel,
        out_shape=jax.ShapeDtypeStruct((rows, width), BF16),
        in_specs=[vmem] * 6 + [hbm] * 4,
        out_specs=vmem,
        scratch_shapes=[
            pltpu.VMEM((keys // rows, rows, kv.shape[1]), BF16),
            pltpu.VMEM((rows, keys), F32),
            pltpu.VMEM((rows, H * HD), BF16),
            pltpu.VMEM(w_out.shape, BF16),
            pltpu.VMEM((3, 4 * w_gate.shape[0], width), BF16),
            block,
            block,
            pltpu.VMEM((4, 2, rows, width), BF16),
            pltpu.VMEM((4, rows, width), F32),
            blocks,
            blocks,
            block,
            block,
            block,
            block,
            block,
            block,
            dma((20,)),
            dma((20,)),
            dma((3,)),
            dma((9,)),
            dma((9,)),
            dma((3,)),
            dma((3,)),
            dma((3,)),
            dma((3,)),
            dma((3,)),
            dma((4,)),
            dma((4,)),
        ],
        compiler_params=pltpu.CompilerParams(
            collective_id=2, has_side_effects=True, vmem_limit_bytes=60 * 1024 * 1024
        ),
        cost_estimate=pl.CostEstimate(
            flops=6 * 32 * rows * width * w_gate.shape[0],
            bytes_accessed=100_000_000,
            transcendentals=0,
        ),
    )(
        queries,
        kv,
        tokens,
        group_seg[None, :],
        own_seg[:, None],
        ffn_gain[None, :],
        w_out,
        w_gate,
        w_up,
        w_down,
    )


def attend(queries, kv_all, group_seg, own_seg, row_base):
    rows, keys = queries.shape[0], kv_all.shape[0]
    q_grid = queries.reshape(rows, KVH, H // KVH, HD).transpose(1, 2, 0, 3)
    kv_grid = kv_all.reshape(keys, 2, KVH, HD).transpose(1, 2, 0, 3)
    query_idx = row_base + jnp.arange(rows, dtype=jnp.int32)
    key_idx = jnp.arange(keys, dtype=jnp.int32)
    allowed = (key_idx[None, :] <= query_idx[:, None]) & (group_seg[None, :] == own_seg[:, None])

    def one_head(args):
        q, k, v = args
        scores = jnp.einsum("gqd,cd->gqc", q, k, preferred_element_type=F32) * SCORE_SCALE
        scores = jnp.where(allowed, scores, NEG_FILL)
        weights = jnp.exp(scores - jnp.max(scores, axis=-1, keepdims=True))
        product = jnp.einsum("gqc,cd->gqd", weights.astype(BF16), v, preferred_element_type=F32)
        return product / jnp.sum(weights, axis=-1, keepdims=True)

    heads = lax.map(one_head, (q_grid, kv_grid[0], kv_grid[1]))
    return heads.transpose(2, 0, 1, 3).reshape(rows, H * HD).astype(BF16)


def unit_terms(pieces, gathered):
    gate_part, up_part, down_part = pieces
    contract = (((1,), (1,)), ((), ()))
    gate_act = lax.dot_general(gathered, gate_part, contract, preferred_element_type=jnp.float32)
    up_act = lax.dot_general(gathered, up_part, contract, preferred_element_type=jnp.float32)
    hidden = (jax.nn.silu(gate_act) * up_act).astype(jnp.bfloat16)
    return jnp.dot(hidden, down_part, preferred_element_type=jnp.float32)


def per_device(
    cube,
    hids,
    tokens,
    segment,
    attn_gain,
    w_query,
    w_key,
    w_value,
    q_gain,
    k_gain,
    w_out,
    ffn_gain,
    w_gate,
    w_up,
    w_down,
):
    shard_rows = tokens.shape[0]
    if cube:
        group_seg = seg_gather(segment, hids)
    else:
        group_seg = lax.all_gather(segment, "hid", axis=0, tiled=True)
    row_base = lax.axis_index("hid") * shard_rows
    own_seg = segment
    first = jnp.sum((group_seg[None, :] < own_seg[:, None]).astype(jnp.int32), axis=1)
    positions = row_base + jnp.arange(shard_rows, dtype=jnp.int32) - first
    resid = tokens.astype(jnp.float32)
    normed = rms_scale(resid, attn_gain).astype(jnp.bfloat16)
    q_raw = jnp.dot(normed, w_query, preferred_element_type=jnp.float32).reshape(shard_rows, H, HD)
    k_raw = jnp.dot(normed, w_key, preferred_element_type=jnp.float32).reshape(shard_rows, KVH, HD)
    queries = rotate(rms_scale(q_raw, q_gain), positions).astype(jnp.bfloat16)
    key_heads = (
        rotate(rms_scale(k_raw, k_gain), positions)
        .astype(jnp.bfloat16)
        .reshape(shard_rows, KVH * HD)
    )
    values = jnp.dot(normed, w_value, preferred_element_type=jnp.float32).astype(jnp.bfloat16)
    kv_cache = jnp.concatenate([key_heads, values], axis=1)
    queries = queries.reshape(shard_rows, H * HD)
    if cube:
        mixed = layer(
            queries, kv_cache, tokens, group_seg, own_seg, ffn_gain, w_out, w_gate, w_up, w_down
        )
        return (mixed, kv_cache)
    kv_all = lax.all_gather(kv_cache, "hid", axis=0, tiled=True)
    attended = attend(queries, kv_all, group_seg, own_seg, row_base)
    after_attn = (resid + jnp.dot(attended, w_out, preferred_element_type=jnp.float32)).astype(
        jnp.bfloat16
    )
    after_f32 = lax.optimization_barrier(after_attn).astype(jnp.float32)
    mlp_in = rms_scale(after_f32, ffn_gain).astype(jnp.bfloat16)
    weights = [lax.all_gather(w, "req", axis=0, tiled=True) for w in (w_gate, w_up, w_down)]
    gathered = lax.all_gather(mlp_in, "hid", axis=0, tiled=True)
    unit_sum = unit_terms(weights, gathered)
    own_share = lax.psum_scatter(
        unit_sum.astype(jnp.bfloat16), "hid", scatter_dimension=0, tiled=True
    ).astype(jnp.float32)
    mixed = (after_f32 + own_share).astype(jnp.bfloat16)
    return (mixed, kv_cache)


def solution(mesh):
    placed = (
        P(("req", "hid"), None),
        P(("req", "hid")),
        P(),
        P(),
        P(),
        P(),
        P(),
        P(),
        P(),
        P(),
        P(("req", "hid"), None),
        P(("req", "hid"), None),
        P(("req", "hid"), None),
    )
    cube = mesh.shape["req"] == 4 and mesh.shape["hid"] == 8
    return jax.shard_map(
        functools.partial(per_device, cube, mesh.shape["hid"]),
        mesh=mesh,
        in_specs=placed,
        out_specs=(P(("req", "hid"), None), P(("req", "hid"), None)),
        check_vma=False,
    )
```

time: 213 us -> 167 us (0.78)
  waiting for transfers between devices: 16.9 us -> 0 us
  between operations: 14.7 us -> 0.83 us
  blocking collectives: 13.7 us -> 0 us
  Pallas kernels: 144 us -> 148 us
  matrix products: 10.5 us -> 7.32 us
  local copies, waits for them, and re-layouts: 8.83 us -> 5.69 us
    all_gather x3 -> x0, waiting for transfers between devices: 14.8 us -> none  [per_device(): lax.all_gather(w, 'hid', axis=0, tiled=True, axis_index_groups=lines)]
    unnamed x1 -> x0, blocking collectives: 13.7 us -> none
    unnamed x28 -> x15, local copies, waits for them, and re-layouts: 8.33 us -> 2.4 us
    pallas_call x3 -> x2, Pallas kernels: 144 us -> 148 us  [the longest x1 139 us: layer(): pl.pallas_call(layer_kernel, out_shape=jax.ShapeDtypeStruct((rows, width)...]
    dot_general x1 -> x0, matrix products: 3.44 us -> none  [per_device(): jnp.dot(attended, w_out, preferred_element_type=jnp.float32)]
  transfers between devices with their start and end apart: 3 -> 0, of which waited for: 1 -> 0; matrix products, arithmetic and copies ran while one was open for 8% -> 0% of each run, Pallas kernels for 41% -> 0%
where the time goes in v2:
time: 167 us
  Pallas kernels  148 us (89%)
  matrix products  7.32 us (4%)
  local copies, waits for them, and re-layouts  5.69 us (3%)
  other arithmetic  4.53 us (3%)
    pallas_call x1, Pallas kernels, layer(): pl.pallas_call(layer_kernel, out_shape=jax.ShapeDtypeStruct((rows, width)...  139 us
    pallas_call x1, Pallas kernels, seg_gather(): pl.pallas_call(functools.partial(seg_gather_kernel, hids), out_shape=jax....  9.57 us
    dot_general x1, matrix products, per_device(): jnp.dot(normed, w_query, preferred_element_type=jnp.float32)  4.6 us

profile of v2, /device:TPU:0, one launch (start us, length us, event | category | flops | bytes accessed | tf_op | source)
XLA Modules:
  0.0 166.5 jit_solution(7386244985468570210)
XLA Ops:
  0.6 1.4 fusion
  2.0 4.6 %fusion.6 = f32[192,1536]{0,1:T(8,128)S(1)} fusion(bf16[1536,1536]{1,0:T(8,128)(2,1)} %param.16, bf16[192,1536]{1,0:T(8,128)(2,1)} %tok_ref.1, f32[1536]{0:T(1024)} %param.15, f32[192]{0:T(256)S(1)} %add_rsqrt_fusion.2), kind=kOutput, calls=%fused_computation.26 | convolution fusion | flops 907149312 | bytes 6494976 | tf_op jit(solution)/shard_map/dot_general | solution.py:522
  6.7 0.2 multiply_reduce_fusion
  6.9 0.4 copy-done.5
  7.3 0.3 multiply_multiply_fusion
  7.7 9.6 %shard_map.140 = s32[8,1,192]{2,1,0:T(1,128)} custom-call(s32[1,192]{1,0:T(1,128)} %bitcast.15), custom_call_target="tpu_custom_call" | custom-call | tf_op jit(solution)/shard_map/pallas_call | solution.py:73
  17.2 0.7 reduce
  18.0 0.1 lt.15
  18.0 0.3 convert_reduce_fusion
  18.3 0.2 multiply_cosine_fusion
  18.5 0.2 subtract_convert_fusion
  18.8 0.1 pad_maximum_fusion
  19.0 1.1 copy.23.q_ref
  20.0 1.9 %convolution_convert_fusion = bf16[192,512]{1,0:T(8,128)(2,1)S(1)} fusion(bf16[1536,512]{1,0:T(8,128)(2,1)} %param.18, bf16[192,1536]{1,0:T(8,128)(2,1)S(1)} %copy-done.1, f32[1536]{0:T(1024)S(1)} %copy-done.6, f32[192]{0:T(256)S(1)} %add_rsqrt_fusion.2), kind=kOutput, calls=%fused_computation.8 | convolution fusion | flops 303267840 | bytes 2366208 | tf_op jit(solution)/shard_map/dot_general | solution.py:530
  22.0 0.8 multiply_reduce_fusion.1
  22.8 0.1 multiply_multiply_fusion.1
  22.9 0.1 subtract_convert_fusion.1
  23.1 0.1 copy.22
  23.2 0.8 pad_maximum_fusion.1.kv_ref
  24.0 0.7 broadcast_in_dim_reshape.4.seg_ref
  24.6 0.8 copy.24.own_ref
  25.4 0.6 broadcast_in_dim.8.gain_ref
  26.0 138.6 %shard_map.141 = bf16[192,1536]{1,0:T(8,128)(2,1)} custom-call(bf16[192,1536]{1,0:T(8,128)(2,1)} %copy.23.q_ref, bf16[192,1024]{1,0:T(8,128)(2,1)} %pad_maximum_fusion.1.kv_ref, bf16[192,1536]{1,0:T(8,128)(2,1)} %tok_ref.1, s32[1,1536]{1,0:T(1,128)} %broadcast_in_dim_reshape.4.seg_ref, s32[192,1]{1,0:T(8,128)} %copy.24.own_ref, ...), custom_call_target="tpu_custom_call" | custom-call | flops 8153726976 | bytes 100000000 | tf_op jit(solution)/shard_map/pallas_call | solution.py:407
  164.6 1.9 %copy.28 = bf16[192,1536]{1,0:T(8,128)(2,1)} copy(bf16[192,1536]{1,0:T(8,128)(2,1)} %shard_map.141) | data formatting | bytes 1179648
  (19 shorter events, 0.1 us)
Async XLA Ops:
  0.6 21.3 %copy-start = (bf16[1536,512]{1,0:T(8,128)(2,1)S(1)}, bf16[1536,512]{1,0:T(8,128)(2,1)}, u32[]{:S(2)}) copy-start(bf16[1536,512]{1,0:T(8,128)(2,1)} %param.17) | copy-start | bytes 4718596
  6.6 0.7 copy-start.5
  7.3 10.7 %copy-start.2 = (s32[192]{0:T(256)S(1)}, s32[192]{0:T(256)}, u32[]{:S(2)}) copy-start(s32[192]{0:T(256)} %param.14) | copy-start | bytes 2308
  18.8 1.3 copy-start.1
  18.8 1.2 copy-start.6
  22.0 0.8 copy-start.4
  22.9 2.5 %copy-start.3 = (f32[1536]{0:T(1024)S(1)}, f32[1536]{0:T(1024)}, u32[]{:S(2)}) copy-start(f32[1536]{0:T(1024)} %param.22) | copy-start | bytes 18436

commit v3 on v2

--- a/solution.py
+++ b/solution.py
@@ -194,7 +194,6 @@
             def _(s=s):
                 across(z + s).start()
 
-        w_z[s].start()
         w_local[s].start()
         if s == 0:
             q_idx = hid * rows + lax.broadcasted_iota(jnp.int32, (rows, keys), 0)
@@ -214,8 +213,8 @@
         left(z + last, last - 1).wait_recv()
         across(z + last).start()
 
-    w_z[0].wait_recv()
-    w_zy[0].start()
+    for w in range(3):
+        w_z[w].start()
     for zb in range(nz):
         across(zb).wait_recv()
     own_kv.wait()
@@ -245,7 +244,12 @@
                 outs.append((o[:, j * HD : (j + 1) * HD] / total).astype(BF16))
         att[:, q_at] = jnp.concatenate(outs, axis=1)
 
-        @pl.when(i == 1)
+        @pl.when(i == 2)
+        def _():
+            w_z[0].wait_recv()
+            w_zy[0].start()
+
+        @pl.when(i == 3)
         def _():
             w_z[1].wait_recv()
             w_zy[1].start()

time: 167 us -> 160 us (0.958)
  Pallas kernels: 148 us -> 141 us
    pallas_call x1, Pallas kernels: 139 us -> 131 us  [layer(): pl.pallas_call(layer_kernel, out_shape=jax.ShapeDtypeStruct((rows, width)...]
where the time goes in v3:
time: 160 us; the launch traced here: 159 us
  Pallas kernels  141 us (88%)
  matrix products  7.32 us (5%)
  local copies, waits for them, and re-layouts  5.69 us (4%)
  other arithmetic  4.53 us (3%)
    pallas_call x1, Pallas kernels, layer(): pl.pallas_call(layer_kernel, out_shape=jax.ShapeDtypeStruct((rows, width)...  131 us
    pallas_call x1, Pallas kernels, seg_gather(): pl.pallas_call(functools.partial(seg_gather_kernel, hids), out_shape=jax....  9.57 us
    dot_general x1, matrix products, per_device(): jnp.dot(normed, w_query, preferred_element_type=jnp.float32)  4.6 us

profile of v3, /device:TPU:0, one launch (start us, length us, event | category | flops | bytes accessed | tf_op | source)
XLA Modules:
  0.0 159.1 jit_solution(7555101348054064450)
XLA Ops:
  0.6 1.4 fusion
  2.0 4.6 %fusion.6 = f32[192,1536]{0,1:T(8,128)S(1)} fusion(bf16[1536,1536]{1,0:T(8,128)(2,1)} %param.16, bf16[192,1536]{1,0:T(8,128)(2,1)} %tok_ref.1, f32[1536]{0:T(1024)} %param.15, f32[192]{0:T(256)S(1)} %add_rsqrt_fusion.2), kind=kOutput, calls=%fused_computation.26 | convolution fusion | flops 907149312 | bytes 6494976 | tf_op jit(solution)/shard_map/dot_general | solution.py:526
  6.7 0.2 multiply_reduce_fusion
  6.9 0.4 copy-done.5
  7.3 0.3 multiply_multiply_fusion
  7.7 9.6 %shard_map.140 = s32[8,1,192]{2,1,0:T(1,128)} custom-call(s32[1,192]{1,0:T(1,128)} %bitcast.15), custom_call_target="tpu_custom_call" | custom-call | tf_op jit(solution)/shard_map/pallas_call | solution.py:73
  17.2 0.7 reduce
  18.0 0.1 lt.15
  18.0 0.3 convert_reduce_fusion
  18.3 0.2 multiply_cosine_fusion
  18.5 0.2 subtract_convert_fusion
  18.8 0.1 pad_maximum_fusion
  19.0 1.1 copy.23.q_ref
  20.0 1.9 %convolution_convert_fusion = bf16[192,512]{1,0:T(8,128)(2,1)S(1)} fusion(bf16[1536,512]{1,0:T(8,128)(2,1)} %param.18, bf16[192,1536]{1,0:T(8,128)(2,1)S(1)} %copy-done.1, f32[1536]{0:T(1024)S(1)} %copy-done.6, f32[192]{0:T(256)S(1)} %add_rsqrt_fusion.2), kind=kOutput, calls=%fused_computation.8 | convolution fusion | flops 303267840 | bytes 2366208 | tf_op jit(solution)/shard_map/dot_general | solution.py:534
  22.0 0.8 multiply_reduce_fusion.1
  22.8 0.1 multiply_multiply_fusion.1
  22.9 0.1 subtract_convert_fusion.1
  23.1 0.1 copy.22
  23.2 0.8 pad_maximum_fusion.1.kv_ref
  24.0 0.7 broadcast_in_dim_reshape.4.seg_ref
  24.6 0.8 copy.24.own_ref
  25.4 0.6 broadcast_in_dim.8.gain_ref
  26.0 131.2 %shard_map.141 = bf16[192,1536]{1,0:T(8,128)(2,1)} custom-call(bf16[192,1536]{1,0:T(8,128)(2,1)} %copy.23.q_ref, bf16[192,1024]{1,0:T(8,128)(2,1)} %pad_maximum_fusion.1.kv_ref, bf16[192,1536]{1,0:T(8,128)(2,1)} %tok_ref.1, s32[1,1536]{1,0:T(1,128)} %broadcast_in_dim_reshape.4.seg_ref, s32[192,1]{1,0:T(8,128)} %copy.24.own_ref, ...), custom_call_target="tpu_custom_call" | custom-call | flops 8153726976 | bytes 100000000 | tf_op jit(solution)/shard_map/pallas_call | solution.py:411
  157.2 1.9 %copy.28 = bf16[192,1536]{1,0:T(8,128)(2,1)} copy(bf16[192,1536]{1,0:T(8,128)(2,1)} %shard_map.141) | data formatting | bytes 1179648
  (19 shorter events, 0.1 us)
Async XLA Ops:
  0.6 21.3 %copy-start = (bf16[1536,512]{1,0:T(8,128)(2,1)S(1)}, bf16[1536,512]{1,0:T(8,128)(2,1)}, u32[]{:S(2)}) copy-start(bf16[1536,512]{1,0:T(8,128)(2,1)} %param.17) | copy-start | bytes 4718596
  6.6 0.7 copy-start.5
  7.3 10.7 %copy-start.2 = (s32[192]{0:T(256)S(1)}, s32[192]{0:T(256)}, u32[]{:S(2)}) copy-start(s32[192]{0:T(256)} %param.14) | copy-start | bytes 2308
  18.8 1.3 copy-start.1
  18.8 1.2 copy-start.6
  22.0 0.8 copy-start.4
  22.9 2.5 %copy-start.3 = (f32[1536]{0:T(1024)S(1)}, f32[1536]{0:T(1024)}, u32[]{:S(2)}) copy-start(f32[1536]{0:T(1024)} %param.22) | copy-start | bytes 18436
